TPU v7x, 256 devices: a whole 4x4x8 slice. The times are simulated.
256 devices in a mesh: vert: 128 (over z, y, x), qcol: 2 (over core).
Axes of the slice: x: 4, y: 4, z: 8, core: 2. Of those that a mesh axis runs over, the one named last changes fastest.
Arguments:
- descriptors: bfloat16 [262144, 2048], P('vert'), may hold values from -0.8984375 to 0.8984375
- queries: bfloat16 [512, 2048], P('qcol', 'vert'), may hold values from -0.8984375 to 0.8984375
- tiles: bfloat16 [6144, 128, 128], P('vert'), may hold values from 0 to 1, as said below
- tile_cols: int32 [128, 3, 16], replicated, may hold values from 0 to 15, as said below
- part_size: int32 [128], replicated, may hold values from 1024 to 2048, as said below
Outputs:
- ranking: float32 [262144, 512], P('vert', 'qcol')
- residual: float32 [262144, 512], P('vert', 'qcol')
Inputs may be any that keep to these rules, and one draw needn't show every extreme that they name: For each part d and slot j, tile_cols[d, j, :] is a permutation of 0 to 15. `part_size`: some part has exactly 2048 live vertices and some exactly 1024. tiles are sparse and nonnegative; every row and every column of B sums to at most 1.01.
All inputs are finite; a program needn't handle non-finite values.
Results may differ from a plain program's by a relative error of at most 0.0003.
Values may be sent and summed in bfloat16 or wider, within the bound.
A program may use at most 128 MiB of HBM per device.

v0:
```python
import jax
import jax.numpy as jnp
from jax import lax
from jax.sharding import PartitionSpec as P

ITERS = 2


def padded(block, sides, width):
    for axis, dim in sides:
        count = lax.axis_size(axis)
        forward = [(i, i + 1) for i in range(count - 1)]
        forward.append((count - 1, 0))
        backward = [(target, source) for source, target in forward]
        low = lax.ppermute(
            lax.slice_in_dim(block, block.shape[dim] - width, None, axis=dim), axis, forward
        )
        high = lax.ppermute(lax.slice_in_dim(block, 0, width, axis=dim), axis, backward)
        block = jnp.concatenate([low, block, high], axis=dim)
    return block


def shifted(x, axis, by):
    peers = lax.axis_size(axis)
    return lax.ppermute(x, axis, [(i, (i + by) % peers) for i in range(peers)])


def transposed(blocks_slot, rows3, cols_row):
    moved = jnp.einsum("rba,rbq->raq", blocks_slot, rows3, precision=lax.Precision.HIGHEST)
    return moved[jnp.argsort(cols_row)]


def body(descriptors, queries, tiles, tile_cols, part_size):
    rows = descriptors.shape[0]
    qdev = queries.shape[0]
    tile = tiles.shape[1]
    rtiles = rows // tile
    slots = tiles.shape[0] // rtiles
    here = lax.axis_index("vert")
    sims = lax.dot_general(
        descriptors,
        lax.all_gather(queries, "vert", axis=1, tiled=True),
        (((1,), (1,)), ((), ())),
        preferred_element_type=jnp.float32,
    )
    live_count = lax.dynamic_index_in_dim(part_size, here, 0, keepdims=False)
    live = (lax.iota(jnp.int32, rows) < live_count).astype(jnp.float32)[:, None]
    seeds = live * jnp.maximum(sims, 0.0) ** 3
    blocks = tiles.astype(jnp.float32).reshape(slots, rtiles, tile, tile)
    own_cols = lax.dynamic_index_in_dim(tile_cols, here, 0, keepdims=False)

    def squares(values):
        return lax.psum(jnp.sum(values * values, axis=0), "vert")

    ranking = jnp.zeros_like(seeds)
    residual = seeds
    direction = seeds
    norm_now = squares(residual)
    for step in range(ITERS):
        widened = padded(direction, (("vert", 0),), rows)
        forward = jnp.zeros((rtiles, tile, qdev), jnp.float32)
        for slot in range(slots):
            source = widened[slot * rows : (slot + 1) * rows].reshape(rtiles, tile, qdev)
            picked = source[own_cols[slot]]
            forward = forward + jnp.einsum(
                "rab,rbq->raq", blocks[slot], picked, precision=lax.Precision.HIGHEST
            )
        own3 = direction.reshape(rtiles, tile, qdev)
        middle = transposed(blocks[1], own3, own_cols[1])
        toward_low = transposed(blocks[0], own3, own_cols[0])
        toward_high = transposed(blocks[slots - 1], own3, own_cols[slots - 1])
        back = middle + shifted(toward_low, "vert", -1) + shifted(toward_high, "vert", 1)
        both = (forward + back).reshape(rows, qdev)
        image = direction - 0.99 * live * (0.5 * both)
        curve = lax.psum(jnp.sum(direction * image, axis=0), "vert")
        alpha = norm_now / curve
        ranking = ranking + alpha[None, :] * direction
        residual = residual - alpha[None, :] * image
        norm_next = squares(residual)
        direction = residual + (norm_next / norm_now)[None, :] * direction
        norm_now = norm_next
    return (ranking, residual)


def solution(mesh):
    placed = (P("vert", None), P("qcol", "vert"), P("vert", None, None), P(), P())
    return jax.shard_map(
        body,
        mesh=mesh,
        in_specs=placed,
        out_specs=(P("vert", "qcol"), P("vert", "qcol")),
        check_vma=False,
    )
```

profile of v0, /device:TPU:0, one launch (start us, length us, event | category | flops | bytes accessed | tf_op | source)
XLA Modules:
  0.0 1348.9 jit_solution(10652084589290533953)
XLA Ops:
  7.9 1.3 dynamic_slice.8
  14.6 100.5 %all-gather.2.cloned.1.call-done = bf16[256,2048]{0,1:T(8,128)(2,1)} async-done(((bf16[256,16]{0,1:T(8,128)(2,1)}), bf16[256,2048]{0,1:T(8,128)(2,1)}) %all-gather.2.cloned.1.call-update) | async-done | bytes 1048592 | tf_op jit(solution)/shard_map/all_gather | solution.py:42
  115.1 6.1 fusion
  121.2 1.4 collective-permute-start
  122.6 6.1 collective-permute-start.1
  128.7 4.3 convolution_bitcast_fusion.4
  133.0 2.9 copy.16
  135.9 3.6 gather_fusion.4
  139.5 1.4 collective-permute-start.2
  140.9 4.3 convolution_bitcast_fusion.3
  145.2 2.9 copy.18
  148.1 3.6 gather_fusion.5
  153.1 4.3 convolution_bitcast_fusion.5
  157.4 2.9 copy.14
  160.3 2.0 gather_fusion.1
  162.3 3.6 gather_fusion.3
  165.9 4.1 fusion.17
  170.0 5.3 collective-permute-done
  175.4 3.6 gather_fusion
  179.0 3.7 gather_fusion.2
  182.7 3.0 fusion.23
  185.7 28.8 %collective-permute-done.2 = f32[16,128,256]{2,1,0:T(8,128)} collective-permute-done((f32[16,128,256]{2,1,0:T(8,128)}, f32[16,128,256]{2,1,0:T(8,128)}, u32[]{:S(2)}, u32[]{:S(2)}) %collective-permute-start.2) | collective-permute-done | bytes 2097184 | tf_op jit(solution)/shard_map/ppermute | solution.py:25
  215.2 5.1 bitcast_add_fusion.1
  221.7 349.4 %all-reduce = (f32[256]{0:T(256)S(1)}, f32[256]{0:T(256)S(1)}) all-reduce(f32[256]{0:T(256)S(1)} %get-tuple-element.9, f32[256]{0:T(256)S(1)} %get-tuple-element.8), channel_id=1, replica_groups=mesh['vert'=128,'qcol'=2] {'vert'}, use_global_device_ids=true, to_apply=%region_1.2 | all-reduce | flops 512 | bytes 4096 | tf_op jit(solution)/shard_map/psum | solution.py:53
  571.0 2.1 multiply_reduce_fusion.1
  573.1 343.0 %psum.30 = f32[256]{0:T(256)S(1)} all-reduce(f32[256]{0:T(256)S(1)} %multiply_reduce_fusion.1), channel_id=1, replica_groups=mesh['vert'=128,'qcol'=2] {'vert'}, use_global_device_ids=true, to_apply=%region_8.9 | all-reduce | flops 256 | bytes 2048 | tf_op jit(solution)/shard_map/psum | solution.py:53
  916.1 3.4 multiply_add_fusion.1
  919.5 2.0 collective-permute-start.4
  921.5 5.5 collective-permute-start.5
  927.0 4.9 convolution_bitcast_fusion.1
  932.0 2.9 copy.22
  934.8 3.6 gather_fusion.10
  938.4 5.0 convolution_bitcast_fusion
  943.4 3.0 copy.24
  946.4 3.6 gather_fusion.11
  949.9 2.0 collective-permute-start.7
  952.0 3.6 gather_fusion.7
  955.6 5.0 convolution_bitcast_fusion.2
  960.6 2.9 copy.20
  963.5 3.6 gather_fusion.9
  967.1 4.1 fusion.14
  971.3 3.6 gather_fusion.6
  974.9 3.6 gather_fusion.8
  978.5 3.0 fusion.20
  981.9 5.1 bitcast_add_fusion
  988.4 1.9 multiply_reduce_fusion
  990.3 347.1 %psum.31 = f32[256]{0:T(256)S(1)} all-reduce(f32[256]{0:T(256)S(1)} %multiply_reduce_fusion), channel_id=1, replica_groups=mesh['vert'=128,'qcol'=2] {'vert'}, use_global_device_ids=true, to_apply=%region_10.11 | all-reduce | flops 256 | bytes 2048 | tf_op jit(solution)/shard_map/psum | solution.py:75
  1337.5 4.6 multiply_subtract_fusion
  (46 shorter events, 11.4 us)
Async XLA Ops:
  7.2 107.9 %all-gather.2.cloned.1.call-start = ((), (), s32[]{:S(2)}) async-start(), calls=%async_computation | async-start | bytes 1056768 | tf_op jit(solution)/shard_map/all_gather | solution.py:42
  121.2 54.2 %collective-permute-start = (f32[2048,256]{1,0:T(8,128)S(1)}, f32[2048,256]{1,0:T(8,128)}, u32[]{:S(2)}, u32[]{:S(2)}) collective-permute-start(f32[2048,256]{1,0:T(8,128)S(1)} %fusion), channel_id=1, source_target_pairs={{0,2},{2,4},{4,6},{6,8},{8,10},{10,12},{12,14},{14,16},{16,18},{18... | collective-permute-start | bytes 6291464 | tf_op jit(solution)/shard_map/ppermute | solution.py:15
  122.6 56.4 %collective-permute-start.1 = (f32[2048,256]{1,0:T(8,128)S(1)}, f32[2048,256]{1,0:T(8,128)}, u32[]{:S(2)}, u32[]{:S(2)}) collective-permute-start(f32[2048,256]{1,0:T(8,128)S(1)} %fusion), channel_id=1, source_target_pairs={{2,0},{4,2},{6,4},{8,6},{10,8},{12,10},{14,12},{16,14},{18,16},{20... | collective-permute-start | bytes 6291464 | tf_op jit(solution)/shard_map/ppermute | solution.py:18
  139.5 74.9 %collective-permute-start.2 = (f32[16,128,256]{2,1,0:T(8,128)}, f32[16,128,256]{2,1,0:T(8,128)}, u32[]{:S(2)}, u32[]{:S(2)}) collective-permute-start(f32[16,128,256]{2,1,0:T(8,128)} %gather_fusion.4), channel_id=1, source_target_pairs={{0,254},{2,0},{4,2},{6,4},{8,6},{10,8},{12,10},{14,12},{16,14},{18... | collective-permute-start | bytes 6291464 | tf_op jit(solution)/shard_map/ppermute | solution.py:25
  151.6 63.5 %collective-permute-start.3 = (f32[16,128,256]{2,1,0:T(8,128)}, f32[16,128,256]{2,1,0:T(8,128)}, u32[]{:S(2)}, u32[]{:S(2)}) collective-permute-start(f32[16,128,256]{2,1,0:T(8,128)} %gather_fusion.5), channel_id=1, source_target_pairs={{0,2},{2,4},{4,6},{6,8},{8,10},{10,12},{12,14},{14,16},{16,18},{18... | collective-permute-start | bytes 6291464 | tf_op jit(solution)/shard_map/ppermute | solution.py:25
  182.7 32.5 %copy-start.4 = (f32[16,128,256]{2,1,0:T(8,128)S(1)}, f32[16,128,256]{2,1,0:T(8,128)}, u32[]{:S(2)}) copy-start(f32[16,128,256]{2,1,0:T(8,128)} %gather_fusion.3) | copy-start | bytes 6291460
  182.7 32.5 %copy-start.5 = (f32[16,256,128]{1,2,0:T(8,128)S(1)}, f32[16,256,128]{1,2,0:T(8,128)}, u32[]{:S(2)}) copy-start(f32[16,256,128]{1,2,0:T(8,128)} %fusion.17) | copy-start | bytes 6291460
  220.3 1.4 copy-start
  919.5 51.7 %collective-permute-start.4 = (f32[2048,256]{1,0:T(8,128)}, f32[2048,256]{1,0:T(8,128)}, u32[]{:S(2)}, u32[]{:S(2)}) collective-permute-start(f32[2048,256]{1,0:T(8,128)} %multiply_add_fusion.1), channel_id=1, source_target_pairs={{0,2},{2,4},{4,6},{6,8},{8,10},{10,12},{12,14},{14,16},{16,18},{18... | collective-permute-start | bytes 6291464 | tf_op jit(solution)/shard_map/ppermute | solution.py:15
  921.5 53.4 %collective-permute-start.5 = (f32[2048,256]{1,0:T(8,128)}, f32[2048,256]{1,0:T(8,128)}, u32[]{:S(2)}, u32[]{:S(2)}) collective-permute-start(f32[2048,256]{1,0:T(8,128)} %multiply_add_fusion.1), channel_id=1, source_target_pairs={{2,0},{4,2},{6,4},{8,6},{10,8},{12,10},{14,12},{16,14},{18,16},{20... | collective-permute-start | bytes 6291464 | tf_op jit(solution)/shard_map/ppermute | solution.py:18
  938.4 43.0 %collective-permute-start.6 = (f32[16,128,256]{2,1,0:T(8,128)}, f32[16,128,256]{2,1,0:T(8,128)}, u32[]{:S(2)}, u32[]{:S(2)}) collective-permute-start(f32[16,128,256]{2,1,0:T(8,128)} %gather_fusion.10), channel_id=1, source_target_pairs={{0,254},{2,0},{4,2},{6,4},{8,6},{10,8},{12,10},{14,12},{16,14},{18... | collective-permute-start | bytes 6291464 | tf_op jit(solution)/shard_map/ppermute | solution.py:25
  949.9 32.0 %collective-permute-start.7 = (f32[16,128,256]{2,1,0:T(8,128)}, f32[16,128,256]{2,1,0:T(8,128)}, u32[]{:S(2)}, u32[]{:S(2)}) collective-permute-start(f32[16,128,256]{2,1,0:T(8,128)} %gather_fusion.11), channel_id=1, source_target_pairs={{0,2},{2,4},{4,6},{6,8},{8,10},{10,12},{12,14},{14,16},{16,18},{18... | collective-permute-start | bytes 6291464 | tf_op jit(solution)/shard_map/ppermute | solution.py:25
  978.5 3.5 copy-start.2
  978.5 3.5 copy-start.3
  987.1 1.3 copy-start.1
Sparse Core Ops, SparseCore 0:
  11.4 103.6 all-gather.1
where the time goes:
time: 1350 us
  blocking collectives  1040 us (77%)
  waiting for transfers between devices  136 us (10%)
  local copies, waits for them, and re-layouts  63.5 us (5%)
  matrix products  58.4 us (4%)
  starting transfers between devices  19.1 us (1%)
  other arithmetic  17.7 us (1%)
  between operations  14.2 us (1%)
    psum x2, blocking collectives, squares(): return lax.psum(jnp.sum(values * values, axis=0), 'vert')  692 us
    psum x1, blocking collectives, body(): curve = lax.psum(jnp.sum(direction * image, axis=0), 'vert')  347 us
    all_gather x1, waiting for transfers between devices, body(): lax.all_gather(queries, 'vert', axis=1, tiled=True)  100 us
    ppermute x4, waiting for transfers between devices, shifted(): return lax.ppermute(x, axis, [(i, (i + by) % peers) for i in range(peers)])  30 us
    dot_general x6, matrix products, transposed(): jnp.einsum('rba,rbq->raq', blocks_slot, rows3, precision=lax.Precision.HI...  27.8 us
  transfers between devices with their start and end apart: 9, of which 5 were waited for; matrix products, arithmetic and copies ran while one was open for 8% of the time, Pallas kernels for 0%

commit v1 on v0

--- a/solution.py
+++ b/solution.py
@@ -4,6 +4,7 @@
 from jax.sharding import PartitionSpec as P
 
 ITERS = 2
+make_patch = lambda row_data: jnp.sum(lax.all_gather(row_data, axis_name="vert"), axis=0)
 
 
 def padded(block, sides, width):
@@ -72,7 +73,7 @@
         back = middle + shifted(toward_low, "vert", -1) + shifted(toward_high, "vert", 1)
         both = (forward + back).reshape(rows, qdev)
         image = direction - 0.99 * live * (0.5 * both)
-        curve = lax.psum(jnp.sum(direction * image, axis=0), "vert")
+        curve = make_patch(jnp.sum(direction * image, axis=0))
         alpha = norm_now / curve
         ranking = ranking + alpha[None, :] * direction
         residual = residual - alpha[None, :] * image

time: 1350 us -> 1690 us (1.25)
  blocking collectives: 1040 us -> 1380 us
    all_gather x0 -> x2, blocking collectives: none -> 688 us  [lax.all_gather(row_data, axis_name='vert')]
    psum x1 -> x0, blocking collectives: 347 us -> none  [body(): curve = lax.psum(jnp.sum(direction * image, axis=0), 'vert')]
  transfers between devices with their start and end apart: 9 -> 9, of which waited for: 5 -> 5; matrix products, arithmetic and copies ran while one was open for 8% -> 6% of each run, Pallas kernels for 0% -> 0%
where the time goes in v1:
time: 1690 us; the launch traced here: 1680 us
  blocking collectives  1380 us (82%)
  waiting for transfers between devices  136 us (8%)
  local copies, waits for them, and re-layouts  62.3 us (4%)
  matrix products  58.4 us (3%)
  starting transfers between devices  19.1 us (1%)
  other arithmetic  18.7 us (1%)
    all_gather x2, blocking collectives, lax.all_gather(row_data, axis_name='vert')  688 us
    psum x2, blocking collectives, squares(): return lax.psum(jnp.sum(values * values, axis=0), 'vert')  687 us
    all_gather x1, waiting for transfers between devices, body(): lax.all_gather(queries, 'vert', axis=1, tiled=True)  100 us
  transfers between devices with their start and end apart: 9, of which 5 were waited for; matrix products, arithmetic and copies ran while one was open for 6% of the time, Pallas kernels for 0%

profile of v1, /device:TPU:0, one launch (start us, length us, event | category | flops | bytes accessed | tf_op | source)
XLA Modules:
  0.0 1684.5 jit_solution(7018861464725111210)
XLA Ops:
  7.9 1.3 dynamic_slice.8
  14.6 100.5 %all-gather.6.cloned.1.call-done = bf16[256,2048]{0,1:T(8,128)(2,1)} async-done(((bf16[256,16]{0,1:T(8,128)(2,1)}), bf16[256,2048]{0,1:T(8,128)(2,1)}) %all-gather.6.cloned.1.call-update) | async-done | bytes 1048592 | tf_op jit(solution)/shard_map/all_gather | solution.py:43
  115.1 6.1 fusion
  121.2 1.4 collective-permute-start
  122.6 6.1 collective-permute-start.1
  128.7 4.3 convolution_bitcast_fusion.4
  133.0 2.9 copy.28
  135.9 3.6 gather_fusion.4
  139.5 1.4 collective-permute-start.2
  140.9 4.3 convolution_bitcast_fusion.3
  145.2 2.9 copy.30
  148.1 3.6 gather_fusion.5
  153.1 4.3 convolution_bitcast_fusion.5
  157.4 2.9 copy.26
  160.3 2.0 gather_fusion.1
  162.3 3.6 gather_fusion.3
  165.9 4.1 fusion.17
  170.0 5.3 collective-permute-done
  175.4 3.6 gather_fusion
  179.0 3.7 gather_fusion.2
  182.7 3.0 fusion.23
  185.7 28.8 %collective-permute-done.2 = f32[16,128,256]{2,1,0:T(8,128)} collective-permute-done((f32[16,128,256]{2,1,0:T(8,128)}, f32[16,128,256]{2,1,0:T(8,128)}, u32[]{:S(2)}, u32[]{:S(2)}) %collective-permute-start.2) | collective-permute-done | bytes 2097184 | tf_op jit(solution)/shard_map/ppermute | solution.py:26
  215.2 5.1 bitcast_add_fusion.1
  221.7 345.2 %all-gather.2 = f32[128,1,256]{2,1,0:T(1,128)S(1)} all-gather(f32[1,1,256]{2,1,0:T(1,128)S(1)} %bitcast.78), channel_id=2, replica_groups=mesh['vert'=128,'qcol'=2] {'vert'}, dimensions={0}, use_global_device_ids=true | all-gather | bytes 132096 | tf_op jit(solution)/shard_map/all_gather | solution.py:7
  566.8 342.2 %psum.14 = f32[256]{0:T(256)S(1)} all-reduce(f32[256]{0:T(256)S(1)} %get-tuple-element.9), channel_id=1, replica_groups=mesh['vert'=128,'qcol'=2] {'vert'}, use_global_device_ids=true, to_apply=%region_1.2 | all-reduce | flops 256 | bytes 2048 | tf_op jit(solution)/shard_map/psum | solution.py:54
  909.2 2.1 multiply_reduce_fusion.1
  911.3 345.0 %psum.15 = f32[256]{0:T(256)S(1)} all-reduce(f32[256]{0:T(256)S(1)} %multiply_reduce_fusion.1), channel_id=1, replica_groups=mesh['vert'=128,'qcol'=2] {'vert'}, use_global_device_ids=true, to_apply=%region_8.9 | all-reduce | flops 256 | bytes 2048 | tf_op jit(solution)/shard_map/psum | solution.py:54
  1256.3 3.4 multiply_add_fusion.1
  1259.7 7.5 collective-permute-start.5
  1267.1 4.9 convolution_bitcast_fusion.1
  1272.1 2.9 copy.34
  1275.0 3.6 gather_fusion.10
  1278.6 5.0 convolution_bitcast_fusion
  1283.5 3.0 copy.36
  1286.5 3.6 gather_fusion.11
  1290.1 2.0 collective-permute-start.7
  1292.1 3.6 gather_fusion.7
  1295.7 5.0 convolution_bitcast_fusion.2
  1300.7 2.9 copy.32
  1303.6 3.6 gather_fusion.9
  1307.2 4.1 fusion.14
  1311.4 3.6 gather_fusion.6
  1315.0 3.6 gather_fusion.8
  1318.6 3.0 fusion.20
  1321.9 5.1 bitcast_add_fusion
  1327.0 2.7 multiply_reduce_fusion
  1329.8 343.2 %all-gather.3 = f32[128,1,256]{2,1,0:T(1,128)S(1)} all-gather(f32[1,1,256]{2,1,0:T(1,128)S(1)} %bitcast.77), channel_id=3, replica_groups=mesh['vert'=128,'qcol'=2] {'vert'}, dimensions={0}, use_global_device_ids=true | all-gather | bytes 132096 | tf_op jit(solution)/shard_map/all_gather | solution.py:7
  1673.1 4.6 multiply_subtract_fusion
  (49 shorter events, 10.2 us)
Async XLA Ops:
  7.2 107.9 %all-gather.6.cloned.1.call-start = ((), (), s32[]{:S(2)}) async-start(), calls=%async_computation | async-start | bytes 1056768 | tf_op jit(solution)/shard_map/all_gather | solution.py:43
  121.2 54.2 %collective-permute-start = (f32[2048,256]{1,0:T(8,128)S(1)}, f32[2048,256]{1,0:T(8,128)}, u32[]{:S(2)}, u32[]{:S(2)}) collective-permute-start(f32[2048,256]{1,0:T(8,128)S(1)} %fusion), channel_id=1, source_target_pairs={{0,2},{2,4},{4,6},{6,8},{8,10},{10,12},{12,14},{14,16},{16,18},{18... | collective-permute-start | bytes 6291464 | tf_op jit(solution)/shard_map/ppermute | solution.py:16
  122.6 56.4 %collective-permute-start.1 = (f32[2048,256]{1,0:T(8,128)S(1)}, f32[2048,256]{1,0:T(8,128)}, u32[]{:S(2)}, u32[]{:S(2)}) collective-permute-start(f32[2048,256]{1,0:T(8,128)S(1)} %fusion), channel_id=1, source_target_pairs={{2,0},{4,2},{6,4},{8,6},{10,8},{12,10},{14,12},{16,14},{18,16},{20... | collective-permute-start | bytes 6291464 | tf_op jit(solution)/shard_map/ppermute | solution.py:19
  139.5 74.9 %collective-permute-start.2 = (f32[16,128,256]{2,1,0:T(8,128)}, f32[16,128,256]{2,1,0:T(8,128)}, u32[]{:S(2)}, u32[]{:S(2)}) collective-permute-start(f32[16,128,256]{2,1,0:T(8,128)} %gather_fusion.4), channel_id=1, source_target_pairs={{0,254},{2,0},{4,2},{6,4},{8,6},{10,8},{12,10},{14,12},{16,14},{18... | collective-permute-start | bytes 6291464 | tf_op jit(solution)/shard_map/ppermute | solution.py:26
  151.6 63.5 %collective-permute-start.3 = (f32[16,128,256]{2,1,0:T(8,128)}, f32[16,128,256]{2,1,0:T(8,128)}, u32[]{:S(2)}, u32[]{:S(2)}) collective-permute-start(f32[16,128,256]{2,1,0:T(8,128)} %gather_fusion.5), channel_id=1, source_target_pairs={{0,2},{2,4},{4,6},{6,8},{8,10},{10,12},{12,14},{14,16},{16,18},{18... | collective-permute-start | bytes 6291464 | tf_op jit(solution)/shard_map/ppermute | solution.py:26
  182.7 32.5 %copy-start.4 = (f32[16,128,256]{2,1,0:T(8,128)S(1)}, f32[16,128,256]{2,1,0:T(8,128)}, u32[]{:S(2)}) copy-start(f32[16,128,256]{2,1,0:T(8,128)} %gather_fusion.3) | copy-start | bytes 6291460
  182.7 32.5 %copy-start.5 = (f32[16,256,128]{1,2,0:T(8,128)S(1)}, f32[16,256,128]{1,2,0:T(8,128)}, u32[]{:S(2)}) copy-start(f32[16,256,128]{1,2,0:T(8,128)} %fusion.17) | copy-start | bytes 6291460
  220.3 1.4 copy-start
  1259.7 51.7 %collective-permute-start.4 = (f32[2048,256]{1,0:T(8,128)}, f32[2048,256]{1,0:T(8,128)}, u32[]{:S(2)}, u32[]{:S(2)}) collective-permute-start(f32[2048,256]{1,0:T(8,128)} %multiply_add_fusion.1), channel_id=1, source_target_pairs={{0,2},{2,4},{4,6},{6,8},{8,10},{10,12},{12,14},{14,16},{16,18},{18... | collective-permute-start | bytes 6291464 | tf_op jit(solution)/shard_map/ppermute | solution.py:16
  1259.7 55.3 %collective-permute-start.5 = (f32[2048,256]{1,0:T(8,128)}, f32[2048,256]{1,0:T(8,128)}, u32[]{:S(2)}, u32[]{:S(2)}) collective-permute-start(f32[2048,256]{1,0:T(8,128)} %multiply_add_fusion.1), channel_id=1, source_target_pairs={{2,0},{4,2},{6,4},{8,6},{10,8},{12,10},{14,12},{16,14},{18,16},{20... | collective-permute-start | bytes 6291464 | tf_op jit(solution)/shard_map/ppermute | solution.py:19
  1278.6 43.0 %collective-permute-start.6 = (f32[16,128,256]{2,1,0:T(8,128)}, f32[16,128,256]{2,1,0:T(8,128)}, u32[]{:S(2)}, u32[]{:S(2)}) collective-permute-start(f32[16,128,256]{2,1,0:T(8,128)} %gather_fusion.10), channel_id=1, source_target_pairs={{0,254},{2,0},{4,2},{6,4},{8,6},{10,8},{12,10},{14,12},{16,14},{18... | collective-permute-start | bytes 6291464 | tf_op jit(solution)/shard_map/ppermute | solution.py:26
  1290.1 31.8 %collective-permute-start.7 = (f32[16,128,256]{2,1,0:T(8,128)}, f32[16,128,256]{2,1,0:T(8,128)}, u32[]{:S(2)}, u32[]{:S(2)}) collective-permute-start(f32[16,128,256]{2,1,0:T(8,128)} %gather_fusion.11), channel_id=1, source_target_pairs={{0,2},{2,4},{4,6},{6,8},{8,10},{10,12},{12,14},{14,16},{16,18},{18... | collective-permute-start | bytes 6291464 | tf_op jit(solution)/shard_map/ppermute | solution.py:26
  1318.6 3.3 copy-start.2
  1318.6 3.3 copy-start.3
  1327.0 2.7 copy-start.1
Sparse Core Ops, SparseCore 0:
  11.4 103.6 all-gather.5
